TPU v7x, 128 devices: a whole 4x4x4 slice. The times are simulated.
128 devices in a mesh: mem: 32 (over z, y, core), band: 4 (over x).
Axes of the slice: x: 4, y: 4, z: 4, core: 2. Of those that a mesh axis runs over, the one named last changes fastest.
Arguments:
- ensemble: float32 [256, 1024, 256], P('mem', 'band'), may hold values from -8 to 8
- column_operator: float32 [128, 128], replicated, may hold values from -0.5 to 0.5
- patch_order: int32 [4, 256], P('band'), may hold values from 0 to 255, as said below
- obs_index: int32 [4, 256, 512], P('band'), may hold values from 0 to 255
- obs_count: int32 [4, 256], P('band', 'mem'), may hold values from 1 to 512
- obs_values: float32 [4, 256, 512], P('band', 'mem'), may hold values from -8 to 8
- obs_precision: float32 [4, 256, 512], P('band', 'mem'), may hold values from 2 to 50
Outputs:
- analysis: float32 [256, 1024, 256], P('mem', 'band')
- transform: float32 [4, 256, 256, 256], P('band', 'mem')
Inputs may be any that keep to these rules, and one draw needn't show every extreme that they name: `patch_order`: each row is a permutation of 0 to 255.
All inputs are finite; a program needn't handle non-finite values.
Results may differ from a plain program's by a relative error of at most 0.0003.
Values sent between devices are 32-bit elements; how exact they have to be, the bound alone decides.
No kernel may reach another device: no remote copies, remote signals or barrier semaphores. Data moves between devices by JAX's collectives and lax.ppermute only.
A program may use at most 64 MiB of HBM per device.

v0:
```python
import math

import jax
import jax.numpy as jnp
from jax import lax
from jax.sharding import PartitionSpec as P

ITERS = 12


def batched(left, right):
    return jnp.einsum("pij,pjk->pik", left, right, precision=lax.Precision.HIGHEST)


def map_columns(states, column_operator):
    rows, patches, cells = states.shape
    levels = column_operator.shape[0]
    flat_rows = states.reshape(rows * patches * (cells // levels), levels)
    mapped = jnp.dot(flat_rows, column_operator, precision=lax.Precision.HIGHEST)
    return mapped.reshape(rows, patches, -1)


def select_slots(channel_values, index):
    width = channel_values.shape[2]
    places = jnp.arange(width, dtype=jnp.int32)
    picker = (index[:, None, :] == places[None, :, None]).astype(jnp.float32)
    return jnp.einsum("kpc,pco->kpo", channel_values, picker, precision=lax.Precision.HIGHEST)


def local(ensemble, column_operator, patch_order, obs_index, obs_count, obs_values, obs_precision):
    highest = lax.Precision.HIGHEST
    members_dev, band_patches, cells = ensemble.shape
    slots = obs_index.shape[2]
    n_mem = lax.axis_size("mem")
    worker = lax.axis_index("mem")
    per_worker = band_patches // n_mem
    order = patch_order[0]
    positions = jnp.arange(band_patches, dtype=jnp.int32)
    permuter = (order[None, :] == positions[:, None]).astype(jnp.float32)
    listed = jnp.einsum("kqc,qj->kjc", ensemble, permuter, precision=highest)
    my_index = lax.dynamic_slice_in_dim(obs_index[0], worker * per_worker, per_worker, 0)
    state_in = lax.all_to_all(listed, "mem", split_axis=1, concat_axis=0, tiled=True)
    obs_block = select_slots(map_columns(state_in, column_operator), my_index)
    count = obs_count[0]
    values = obs_values[0]
    precision = obs_precision[0]
    members = obs_block.shape[0]
    live = (jnp.arange(slots, dtype=jnp.int32)[None, :] < count[:, None]).astype(jnp.float32)
    obs_weight = precision * live
    obs_mean = jnp.mean(obs_block, axis=0)
    obs_pert = obs_block - obs_mean
    innov = (values - obs_mean) * obs_weight
    gram = jnp.einsum("kpo,jpo->pkj", obs_pert * obs_weight, obs_pert, precision=highest)
    identity = jnp.eye(members, dtype=jnp.float32)
    system = gram + (members - 1.0) * identity
    trace_value = jnp.trace(system, axis1=1, axis2=2)
    level = system / trace_value[:, None, None]

    def sweep(step, carry):
        ymat, zmat = carry
        turn = 1.5 * identity - 0.5 * batched(zmat, ymat)
        return (batched(ymat, turn), batched(turn, zmat))

    ymat, zmat = lax.fori_loop(0, ITERS, sweep, (level, jnp.broadcast_to(identity, level.shape)))
    root = zmat / jnp.sqrt(trace_value)[:, None, None]
    spread = math.sqrt(members - 1.0) * root
    projected = jnp.einsum("kpo,po->pk", obs_pert, innov, precision=highest)
    inner = jnp.einsum("pij,pj->pi", root, projected, precision=highest)
    mean_weight = jnp.einsum("pij,pj->pi", root, inner, precision=highest)
    coef = spread + mean_weight[:, :, None]
    state_mean = jnp.mean(state_in, axis=0)
    state_pert = state_in - state_mean
    updated = state_mean + jnp.einsum("pjk,jpc->kpc", coef, state_pert, precision=highest)
    returned = lax.all_to_all(updated, "mem", split_axis=0, concat_axis=1, tiled=True)
    restored = jnp.einsum("kjc,qj->kqc", returned, permuter, precision=highest)
    return (restored, spread[None])


def solution(mesh):
    placed = (
        P("mem", "band", None),
        P(),
        P("band", None),
        P("band", None, None),
        P("band", "mem"),
        P("band", "mem", None),
        P("band", "mem", None),
    )
    return jax.shard_map(
        local,
        mesh=mesh,
        in_specs=placed,
        out_specs=(P("mem", "band", None), P("band", "mem", None, None)),
        check_vma=False,
    )
```

profile of v0, /device:TPU:1, one launch (start us, length us, event | category | flops | bytes accessed | tf_op | source)
XLA Modules:
  0.0 292.0 jit_solution(14203002290290832023)
XLA Ops:
  4.2 2.5 copy.41
  6.7 9.8 %all-to-all-start = ((f32[8,256,256]{2,0,1:T(8,128)}), f32[8,256,256]{2,0,1:T(8,128)}, u32[]{:S(2)}, u32[]{:S(2)}) async-start(f32[8,256,256]{2,0,1:T(8,128)} %copy.41), calls=%async_computation | async-start | bytes 4194304 | tf_op jit(solution)/shard_map/all_to_all | solution.py:42
  17.4 27.0 %all-to-all-done = f32[8,256,256]{2,0,1:T(8,128)} async-done(((f32[8,256,256]{2,0,1:T(8,128)}), f32[8,256,256]{2,0,1:T(8,128)}, u32[]{:S(2)}, u32[]{:S(2)}) %all-to-all-start) | async-done | bytes 2097184 | tf_op jit(solution)/shard_map/all_to_all | solution.py:42
  44.4 3.8 %copy.43 = f32[32,8,8,256]{3,2,1,0:T(8,128)} copy(f32[32,8,8,256]{3,1,2,0:T(8,128)} %bitcast.7) | data formatting | bytes 4194304 | tf_op jit(solution)/shard_map/all_to_all | solution.py:42
  50.4 2.6 reshape.71
  53.0 3.2 %bitcast_subtract_fusion.3 = f32[256,8,256]{2,1,0:T(8,128)} fusion(f32[32,8,8,256]{3,2,1,0:T(8,128)} %copy.43, f32[8,256]{1,0:T(8,128)S(1)} %broadcast_multiply_fusion.1), kind=kLoop, calls=%fused_computation.22 | loop fusion | flops 524288 | bytes 4202496 | tf_op jit(solution)/shard_map/sub | solution.py:72
  56.2 3.1 %fusion.53 = f32[4096,128]{1,0:T(8,128)} fusion(f32[4096,128]{1,0:T(8,128)S(1)} %copy-done.3, f32[128,128]{1,0:T(8,128)S(1)} %copy-done.5), kind=kOutput, calls=%fused_computation.70 | convolution fusion | flops 805306368 | bytes 4259840 | tf_op jit(solution)/shard_map/dot_general | solution.py:19
  59.3 2.9 reshape.72
  62.2 4.3 %bitcast_reduce_fusion = (f32[8,512]{1,0:T(8,128)S(1)}, f32[8,512,256]{1,2,0:T(8,128)S(1)}) fusion(f32[256,8,256]{2,1,0:T(8,128)} %reshape.72, s32[8,512]{1,0:T(8,128)S(1)} %dynamic-slice_bitcast_fusion), kind=kOutput, calls=%fused_computation.16 | convolution fusion | flops 3223318528 | bytes 6324224 | tf_op jit(solution)/shard_map/kpc,pco->kpo/dot_general | solution.py:27
  66.6 3.7 %fusion.15 = f32[8,1,256]{2,1,0:T(1,128)S(1)} fusion(f32[8,512,256]{1,2,0:T(8,128)S(1)} %get-tuple-element.54, f32[8,512]{1,0:T(8,128)S(1)} %get-tuple-element.52, f32[8,512,1]{1,0,2:T(8,128)S(1)} %get-tuple-element.51), kind=kOutput, calls=%fused_computation.19 | convolution fusion | flops 13631488 | bytes 4235264 | tf_op jit(solution)/shard_map/kpo,po->pk/dot_general | solution.py:67
  70.3 4.7 %select_reduce_fusion = (f32[8]{0:T(128)S(1)}, f32[8,256,256]{2,1,0:T(8,128)S(1)}) fusion(f32[256,256]{1,0:T(8,128)S(1)} %fusion.41, pred[256,256]{1,0:T(8,128)(4,1)S(1)} %iota_compare_fusion.3, f32[8,512,256]{1,2,0:T(8,128)S(1)} %get-tuple-element.54, f32[8,512]{1,0:T(8,128)S(1)} %get-tuple-element.52, f32[8,512]{1,0:T(8,128)S(1)} %select_bitcast_fusion), kind=kOutput, calls=%fused_computation.30 | convolution fusion | flops 3225944064 | bytes 6651936 | tf_op jit(solution)/shard_map/kpo,jpo->pkj/dot_general | solution.py:53
  76.7 2.9 %copy.46 = f32[8,256,256]{1,2,0:T(8,128)} copy(f32[8,256,256]{2,1,0:T(8,128)} %add_divide_fusion) | data formatting | bytes 4194304
  81.1 157.3 %while.13 = (s32[]{:T(128)}, f32[8,256,256]{1,2,0:T(8,128)}, f32[8,256,256]{2,1,0:T(8,128)}, s32[]{:T(128)}) while((s32[]{:T(128)}, f32[8,256,256]{1,2,0:T(8,128)}, f32[8,256,256]{2,1,0:T(8,128)}, s32[]{:T(128)}) %tuple.32), condition=%wide.region_4.5_spmd.clone, body=%wide.region_3.4_spmd.clone.sunk | while | flops 4834066432 | bytes 36438096 | solution.py:64
  83.6 2.2 fusion.73
  85.8 4.9 %fusion.75 = f32[8,256,256]{1,2,0:T(8,128)} fusion(f32[8,256,256]{1,2,0:T(8,128)S(1)} %copy.103, f32[8,256,256]{2,1,0:T(8,128)S(1)} %fusion.73, f32[256,256]{1,0:T(8,128)S(1)} %fusion.74), kind=kOutput, calls=%fused_computation.4.clone.1 | convolution fusion | flops 1611661312 | bytes 6553600 | tf_op jit(solution)/shard_map/while/body/eval_jaxpr/pij,pjk->pik/dot_general | solution.py:12
  90.7 3.6 %fusion.76 = f32[8,256,256]{2,1,0:T(8,128)} fusion(f32[8,256,256]{2,1,0:T(8,128)S(1)} %copy.104, f32[8,256,256]{2,1,0:T(8,128)S(1)} %fusion.73, f32[256,256]{1,0:T(8,128)S(1)} %fusion.74), kind=kOutput, calls=%fused_computation.2.clone.1 | convolution fusion | flops 1611661312 | bytes 6553600 | tf_op jit(solution)/shard_map/while/body/eval_jaxpr/pij,pjk->pik/dot_general | solution.py:12
  96.7 2.2 fusion.73
  98.9 4.9 %fusion.75 = f32[8,256,256]{1,2,0:T(8,128)} fusion(f32[8,256,256]{1,2,0:T(8,128)S(1)} %copy.103, f32[8,256,256]{2,1,0:T(8,128)S(1)} %fusion.73, f32[256,256]{1,0:T(8,128)S(1)} %fusion.74), kind=kOutput, calls=%fused_computation.4.clone.1 | convolution fusion | flops 1611661312 | bytes 6553600 | tf_op jit(solution)/shard_map/while/body/eval_jaxpr/pij,pjk->pik/dot_general | solution.py:12
  103.8 3.6 %fusion.76 = f32[8,256,256]{2,1,0:T(8,128)} fusion(f32[8,256,256]{2,1,0:T(8,128)S(1)} %copy.104, f32[8,256,256]{2,1,0:T(8,128)S(1)} %fusion.73, f32[256,256]{1,0:T(8,128)S(1)} %fusion.74), kind=kOutput, calls=%fused_computation.2.clone.1 | convolution fusion | flops 1611661312 | bytes 6553600 | tf_op jit(solution)/shard_map/while/body/eval_jaxpr/pij,pjk->pik/dot_general | solution.py:12
  109.8 2.2 fusion.73
  112.0 4.9 %fusion.75 = f32[8,256,256]{1,2,0:T(8,128)} fusion(f32[8,256,256]{1,2,0:T(8,128)S(1)} %copy.103, f32[8,256,256]{2,1,0:T(8,128)S(1)} %fusion.73, f32[256,256]{1,0:T(8,128)S(1)} %fusion.74), kind=kOutput, calls=%fused_computation.4.clone.1 | convolution fusion | flops 1611661312 | bytes 6553600 | tf_op jit(solution)/shard_map/while/body/eval_jaxpr/pij,pjk->pik/dot_general | solution.py:12
  116.9 3.6 %fusion.76 = f32[8,256,256]{2,1,0:T(8,128)} fusion(f32[8,256,256]{2,1,0:T(8,128)S(1)} %copy.104, f32[8,256,256]{2,1,0:T(8,128)S(1)} %fusion.73, f32[256,256]{1,0:T(8,128)S(1)} %fusion.74), kind=kOutput, calls=%fused_computation.2.clone.1 | convolution fusion | flops 1611661312 | bytes 6553600 | tf_op jit(solution)/shard_map/while/body/eval_jaxpr/pij,pjk->pik/dot_general | solution.py:12
  125.1 4.9 %fusion.75 = f32[8,256,256]{1,2,0:T(8,128)} fusion(f32[8,256,256]{1,2,0:T(8,128)S(1)} %copy.103, f32[8,256,256]{2,1,0:T(8,128)S(1)} %fusion.73, f32[256,256]{1,0:T(8,128)S(1)} %fusion.74), kind=kOutput, calls=%fused_computation.4.clone.1 | convolution fusion | flops 1611661312 | bytes 6553600 | tf_op jit(solution)/shard_map/while/body/eval_jaxpr/pij,pjk->pik/dot_general | solution.py:12
  130.0 3.6 %fusion.76 = f32[8,256,256]{2,1,0:T(8,128)} fusion(f32[8,256,256]{2,1,0:T(8,128)S(1)} %copy.104, f32[8,256,256]{2,1,0:T(8,128)S(1)} %fusion.73, f32[256,256]{1,0:T(8,128)S(1)} %fusion.74), kind=kOutput, calls=%fused_computation.2.clone.1 | convolution fusion | flops 1611661312 | bytes 6553600 | tf_op jit(solution)/shard_map/while/body/eval_jaxpr/pij,pjk->pik/dot_general | solution.py:12
  138.2 4.9 %fusion.75 = f32[8,256,256]{1,2,0:T(8,128)} fusion(f32[8,256,256]{1,2,0:T(8,128)S(1)} %copy.103, f32[8,256,256]{2,1,0:T(8,128)S(1)} %fusion.73, f32[256,256]{1,0:T(8,128)S(1)} %fusion.74), kind=kOutput, calls=%fused_computation.4.clone.1 | convolution fusion | flops 1611661312 | bytes 6553600 | tf_op jit(solution)/shard_map/while/body/eval_jaxpr/pij,pjk->pik/dot_general | solution.py:12
  143.1 3.6 %fusion.76 = f32[8,256,256]{2,1,0:T(8,128)} fusion(f32[8,256,256]{2,1,0:T(8,128)S(1)} %copy.104, f32[8,256,256]{2,1,0:T(8,128)S(1)} %fusion.73, f32[256,256]{1,0:T(8,128)S(1)} %fusion.74), kind=kOutput, calls=%fused_computation.2.clone.1 | convolution fusion | flops 1611661312 | bytes 6553600 | tf_op jit(solution)/shard_map/while/body/eval_jaxpr/pij,pjk->pik/dot_general | solution.py:12
  151.3 4.9 %fusion.75 = f32[8,256,256]{1,2,0:T(8,128)} fusion(f32[8,256,256]{1,2,0:T(8,128)S(1)} %copy.103, f32[8,256,256]{2,1,0:T(8,128)S(1)} %fusion.73, f32[256,256]{1,0:T(8,128)S(1)} %fusion.74), kind=kOutput, calls=%fused_computation.4.clone.1 | convolution fusion | flops 1611661312 | bytes 6553600 | tf_op jit(solution)/shard_map/while/body/eval_jaxpr/pij,pjk->pik/dot_general | solution.py:12
  156.2 3.6 %fusion.76 = f32[8,256,256]{2,1,0:T(8,128)} fusion(f32[8,256,256]{2,1,0:T(8,128)S(1)} %copy.104, f32[8,256,256]{2,1,0:T(8,128)S(1)} %fusion.73, f32[256,256]{1,0:T(8,128)S(1)} %fusion.74), kind=kOutput, calls=%fused_computation.2.clone.1 | convolution fusion | flops 1611661312 | bytes 6553600 | tf_op jit(solution)/shard_map/while/body/eval_jaxpr/pij,pjk->pik/dot_general | solution.py:12
  164.4 4.9 %fusion.75 = f32[8,256,256]{1,2,0:T(8,128)} fusion(f32[8,256,256]{1,2,0:T(8,128)S(1)} %copy.103, f32[8,256,256]{2,1,0:T(8,128)S(1)} %fusion.73, f32[256,256]{1,0:T(8,128)S(1)} %fusion.74), kind=kOutput, calls=%fused_computation.4.clone.1 | convolution fusion | flops 1611661312 | bytes 6553600 | tf_op jit(solution)/shard_map/while/body/eval_jaxpr/pij,pjk->pik/dot_general | solution.py:12
  169.3 3.6 %fusion.76 = f32[8,256,256]{2,1,0:T(8,128)} fusion(f32[8,256,256]{2,1,0:T(8,128)S(1)} %copy.104, f32[8,256,256]{2,1,0:T(8,128)S(1)} %fusion.73, f32[256,256]{1,0:T(8,128)S(1)} %fusion.74), kind=kOutput, calls=%fused_computation.2.clone.1 | convolution fusion | flops 1611661312 | bytes 6553600 | tf_op jit(solution)/shard_map/while/body/eval_jaxpr/pij,pjk->pik/dot_general | solution.py:12
  175.3 2.2 fusion.73
  177.5 4.9 %fusion.75 = f32[8,256,256]{1,2,0:T(8,128)} fusion(f32[8,256,256]{1,2,0:T(8,128)S(1)} %copy.103, f32[8,256,256]{2,1,0:T(8,128)S(1)} %fusion.73, f32[256,256]{1,0:T(8,128)S(1)} %fusion.74), kind=kOutput, calls=%fused_computation.4.clone.1 | convolution fusion | flops 1611661312 | bytes 6553600 | tf_op jit(solution)/shard_map/while/body/eval_jaxpr/pij,pjk->pik/dot_general | solution.py:12
  182.4 3.6 %fusion.76 = f32[8,256,256]{2,1,0:T(8,128)} fusion(f32[8,256,256]{2,1,0:T(8,128)S(1)} %copy.104, f32[8,256,256]{2,1,0:T(8,128)S(1)} %fusion.73, f32[256,256]{1,0:T(8,128)S(1)} %fusion.74), kind=kOutput, calls=%fused_computation.2.clone.1 | convolution fusion | flops 1611661312 | bytes 6553600 | tf_op jit(solution)/shard_map/while/body/eval_jaxpr/pij,pjk->pik/dot_general | solution.py:12
  190.6 4.9 %fusion.75 = f32[8,256,256]{1,2,0:T(8,128)} fusion(f32[8,256,256]{1,2,0:T(8,128)S(1)} %copy.103, f32[8,256,256]{2,1,0:T(8,128)S(1)} %fusion.73, f32[256,256]{1,0:T(8,128)S(1)} %fusion.74), kind=kOutput, calls=%fused_computation.4.clone.1 | convolution fusion | flops 1611661312 | bytes 6553600 | tf_op jit(solution)/shard_map/while/body/eval_jaxpr/pij,pjk->pik/dot_general | solution.py:12
  195.6 3.6 %fusion.76 = f32[8,256,256]{2,1,0:T(8,128)} fusion(f32[8,256,256]{2,1,0:T(8,128)S(1)} %copy.104, f32[8,256,256]{2,1,0:T(8,128)S(1)} %fusion.73, f32[256,256]{1,0:T(8,128)S(1)} %fusion.74), kind=kOutput, calls=%fused_computation.2.clone.1 | convolution fusion | flops 1611661312 | bytes 6553600 | tf_op jit(solution)/shard_map/while/body/eval_jaxpr/pij,pjk->pik/dot_general | solution.py:12
  203.8 4.9 %fusion.75 = f32[8,256,256]{1,2,0:T(8,128)} fusion(f32[8,256,256]{1,2,0:T(8,128)S(1)} %copy.103, f32[8,256,256]{2,1,0:T(8,128)S(1)} %fusion.73, f32[256,256]{1,0:T(8,128)S(1)} %fusion.74), kind=kOutput, calls=%fused_computation.4.clone.1 | convolution fusion | flops 1611661312 | bytes 6553600 | tf_op jit(solution)/shard_map/while/body/eval_jaxpr/pij,pjk->pik/dot_general | solution.py:12
  208.7 3.6 %fusion.76 = f32[8,256,256]{2,1,0:T(8,128)} fusion(f32[8,256,256]{2,1,0:T(8,128)S(1)} %copy.104, f32[8,256,256]{2,1,0:T(8,128)S(1)} %fusion.73, f32[256,256]{1,0:T(8,128)S(1)} %fusion.74), kind=kOutput, calls=%fused_computation.2.clone.1 | convolution fusion | flops 1611661312 | bytes 6553600 | tf_op jit(solution)/shard_map/while/body/eval_jaxpr/pij,pjk->pik/dot_general | solution.py:12
  216.9 4.9 %fusion.75 = f32[8,256,256]{1,2,0:T(8,128)} fusion(f32[8,256,256]{1,2,0:T(8,128)S(1)} %copy.103, f32[8,256,256]{2,1,0:T(8,128)S(1)} %fusion.73, f32[256,256]{1,0:T(8,128)S(1)} %fusion.74), kind=kOutput, calls=%fused_computation.4.clone.1 | convolution fusion | flops 1611661312 | bytes 6553600 | tf_op jit(solution)/shard_map/while/body/eval_jaxpr/pij,pjk->pik/dot_general | solution.py:12
  221.8 3.6 %fusion.76 = f32[8,256,256]{2,1,0:T(8,128)} fusion(f32[8,256,256]{2,1,0:T(8,128)S(1)} %copy.104, f32[8,256,256]{2,1,0:T(8,128)S(1)} %fusion.73, f32[256,256]{1,0:T(8,128)S(1)} %fusion.74), kind=kOutput, calls=%fused_computation.2.clone.1 | convolution fusion | flops 1611661312 | bytes 6553600 | tf_op jit(solution)/shard_map/while/body/eval_jaxpr/pij,pjk->pik/dot_general | solution.py:12
  230.0 4.9 %fusion.75 = f32[8,256,256]{1,2,0:T(8,128)} fusion(f32[8,256,256]{1,2,0:T(8,128)S(1)} %copy.103, f32[8,256,256]{2,1,0:T(8,128)S(1)} %fusion.73, f32[256,256]{1,0:T(8,128)S(1)} %fusion.74), kind=kOutput, calls=%fused_computation.4.clone.1 | convolution fusion | flops 1611661312 | bytes 6553600 | tf_op jit(solution)/shard_map/while/body/eval_jaxpr/pij,pjk->pik/dot_general | solution.py:12
  234.9 3.6 %fusion.76 = f32[8,256,256]{2,1,0:T(8,128)} fusion(f32[8,256,256]{2,1,0:T(8,128)S(1)} %copy.104, f32[8,256,256]{2,1,0:T(8,128)S(1)} %fusion.73, f32[256,256]{1,0:T(8,128)S(1)} %fusion.74), kind=kOutput, calls=%fused_computation.2.clone.1 | convolution fusion | flops 1611661312 | bytes 6553600 | tf_op jit(solution)/shard_map/while/body/eval_jaxpr/pij,pjk->pik/dot_general | solution.py:12
  238.5 3.7 %fusion.49 = f32[8,1,256]{2,1,0:T(1,128)S(1)} fusion(f32[8,256,1]{1,0,2:T(8,128)S(1)} %bitcast.90, f32[8,256,256]{2,1,0:T(8,128)} %get-tuple-element.24, f32[8]{0:T(128)S(1)} %sqrt.7), kind=kOutput, calls=%fused_computation.63 | convolution fusion | flops 6815744 | bytes 2113568 | tf_op jit(solution)/shard_map/pij,pj->pi/dot_general | solution.py:68
  244.2 5.9 %add_bitcast_fusion = f32[256,8,256]{0,2,1:T(8,128)} fusion(f32[256,8,256]{2,1,0:T(8,128)S(1)} %copy-done.4, f32[8,256]{1,0:T(8,128)S(1)} %bitcast.91, f32[8,256]{1,0:T(8,128)S(1)} %broadcast_multiply_fusion.1, f32[8,256,256]{2,1,0:T(8,128)S(1)} %copy-done.2, f32[8]{0:T(128)S(1)} %sqrt.7), kind=kOutput, calls=%fused_computation.28 | convolution fusion | flops 1612709888 | bytes 6307872 | tf_op jit(solution)/shard_map/pjk,jpc->kpc/dot_general | solution.py:73
  250.1 3.1 %copy.48 = f32[256,8,256]{2,1,0:T(8,128)} copy(f32[256,8,256]{0,2,1:T(8,128)} %add_bitcast_fusion) | data formatting | bytes 4194304 | tf_op jit(solution)/shard_map/add | solution.py:73
  253.1 6.7 %all-to-all-start.1 = ((f32[256,8,256]{2,1,0:T(8,128)}), f32[256,8,256]{2,1,0:T(8,128)}, u32[]{:S(2)}, u32[]{:S(2)}) async-start(f32[256,8,256]{2,1,0:T(8,128)} %copy.48), calls=%async_computation.1 | async-start | bytes 4194304 | tf_op jit(solution)/shard_map/all_to_all | solution.py:74
  259.9 3.2 %multiply_bitcast_fusion = f32[1,8,256,256]{3,2,1,0:T(8,128)} fusion(f32[8,256,256]{2,1,0:T(8,128)} %get-tuple-element.24, f32[8]{0:T(128)S(1)} %sqrt.7), kind=kLoop, calls=%fused_computation.35 | loop fusion | flops 1048576 | bytes 4194336 | tf_op jit(solution)/shard_map/broadcast_in_dim | solution.py:76
  263.1 24.7 %all-to-all-done.1 = f32[256,8,256]{2,1,0:T(8,128)} async-done(((f32[256,8,256]{2,1,0:T(8,128)}), f32[256,8,256]{2,1,0:T(8,128)}, u32[]{:S(2)}, u32[]{:S(2)}) %all-to-all-start.1) | async-done | bytes 2097184 | tf_op jit(solution)/shard_map/all_to_all | solution.py:74
  287.9 4.1 %fusion.32 = f32[8,256,256]{2,1,0:T(8,128)} fusion(f32[8,32,8,256]{3,2,0,1:T(8,128)} %bitcast.24, s32[256]{0:T(256)S(1)} %bitcast.94), kind=kOutput, calls=%fused_computation.38 | convolution fusion | flops 1610678272 | bytes 4195328 | tf_op jit(solution)/shard_map/kjc,qj->kqc/dot_general | solution.py:75
  (102 shorter events, 58.6 us)
Async XLA Ops:
  0.6 1.6 copy-start
  6.7 10.6 %copy-start.6 = (f32[1,8,512]{2,1,0:T(8,128)S(1)}, f32[1,8,512]{2,1,0:T(8,128)}, u32[]{:S(2)}) copy-start(f32[1,8,512]{2,1,0:T(8,128)} %param.15) | copy-start | bytes 49156
  6.7 10.6 %copy-start.9 = (s32[1,8]{1,0:T(1,128)S(1)}, s32[1,8]{1,0:T(1,128)}, u32[]{:S(2)}) copy-start(s32[1,8]{1,0:T(1,128)} %param.13) | copy-start | bytes 100
  6.7 37.7 %all-to-all-start = ((f32[8,256,256]{2,0,1:T(8,128)}), f32[8,256,256]{2,0,1:T(8,128)}, u32[]{:S(2)}, u32[]{:S(2)}) async-start(f32[8,256,256]{2,0,1:T(8,128)} %copy.41), calls=%async_computation | async-start | bytes 4194304 | tf_op jit(solution)/shard_map/all_to_all | solution.py:42
  53.0 3.2 %copy-start.3 = (f32[4096,128]{1,0:T(8,128)S(1)}, f32[4096,128]{1,0:T(8,128)}, u32[]{:S(2)}) copy-start(f32[4096,128]{1,0:T(8,128)} %reshape.71) | copy-start | bytes 6291460
  53.0 3.2 %copy-start.5 = (f32[128,128]{1,0:T(8,128)S(1)}, f32[128,128]{1,0:T(8,128)}, u32[]{:S(2)}) copy-start(f32[128,128]{1,0:T(8,128)} %param.10) | copy-start | bytes 196612
  62.2 4.3 %copy-start.7 = (f32[1,8,512]{2,1,0:T(8,128)S(1)}, f32[1,8,512]{2,1,0:T(8,128)}, u32[]{:S(2)}) copy-start(f32[1,8,512]{2,1,0:T(8,128)} %param.14) | copy-start | bytes 49156
  81.1 2.2 copy-start.1
  94.2 2.2 copy-start.1
  107.3 2.2 copy-start.1
  120.4 2.2 copy-start.1
  133.6 2.2 copy-start.1
  146.7 2.2 copy-start.1
  159.8 2.2 copy-start.1
  172.9 2.2 copy-start.1
  186.0 2.2 copy-start.1
  199.1 2.2 copy-start.1
  212.2 2.2 copy-start.1
  225.3 2.2 copy-start.1
  238.5 3.7 %copy-start.2 = (f32[8,256,256]{2,1,0:T(8,128)S(1)}, f32[8,256,256]{2,1,0:T(8,128)}, u32[]{:S(2)}) copy-start(f32[8,256,256]{2,1,0:T(8,128)} %get-tuple-element.24) | copy-start | bytes 6291460
  242.2 2.0 copy-start.4
  253.1 34.7 %all-to-all-start.1 = ((f32[256,8,256]{2,1,0:T(8,128)}), f32[256,8,256]{2,1,0:T(8,128)}, u32[]{:S(2)}, u32[]{:S(2)}) async-start(f32[256,8,256]{2,1,0:T(8,128)} %copy.48), calls=%async_computation.1 | async-start | bytes 4194304 | tf_op jit(solution)/shard_map/all_to_all | solution.py:74
  259.9 28.0 %copy-start.8 = (s32[1,256]{1,0:T(1,128)S(1)}, s32[1,256]{1,0:T(1,128)}, u32[]{:S(2)}) copy-start(s32[1,256]{1,0:T(1,128)} %param.11) | copy-start | bytes 3076
where the time goes:
time: 294 us; the launch traced here: 292 us
  matrix products  161 us (55%)
  waiting for transfers between devices  51.7 us (18%)
  local copies, waits for them, and re-layouts  51 us (17%)
  starting transfers between devices  16.5 us (6%)
  other arithmetic  10.7 us (4%)
    dot_general x36, matrix products, batched(): jnp.einsum('pij,pjk->pik', left, right, precision=lax.Precision.HIGHEST)  128 us
    while x48, local copies, waits for them, and re-layouts  29.3 us
    all_to_all x1, waiting for transfers between devices, local(): lax.all_to_all(listed, 'mem', split_axis=1, concat_axis=0, tiled=True)  27 us
    all_to_all x1, waiting for transfers between devices, local(): lax.all_to_all(updated, 'mem', split_axis=0, concat_axis=1, tiled=True)  24.7 us
    all_to_all x1, starting transfers between devices, local(): lax.all_to_all(listed, 'mem', split_axis=1, concat_axis=0, tiled=True)  9.8 us
    all_to_all x1, starting transfers between devices, local(): lax.all_to_all(updated, 'mem', split_axis=0, concat_axis=1, tiled=True)  6.72 us
  transfers between devices with their start and end apart: 2, of which 2 were waited for; matrix products, arithmetic and copies ran while one was open for 1% of the time, Pallas kernels for 0%

commit v1 on v0

v1 whole, which is shorter than its diff:
```python
import functools
import math

import jax
import jax.numpy as jnp
from jax import lax
from jax.experimental import pallas as pl
from jax.experimental.pallas import tpu as pltpu
from jax.sharding import PartitionSpec as P

F = jnp.float32
BF = jnp.bfloat16
CHUNKS = 1
LOCKSTEP = 4
LANES = 128
VMEM = 56 * 2**20


def split(value, pieces):
    out = []
    for _ in range(pieces):
        head = value.astype(BF)
        out.append(head)
        value = value - head.astype(F)
    return out


def dot(left, right):
    return jnp.dot(left, right, preferred_element_type=F)


def dot_t(left, right):
    return lax.dot_general(left, right, (((1,), (1,)), ((), ())), preferred_element_type=F)


def product(left, right, mul=dot):
    low = mul(left[0], right[1]) + mul(left[1], right[0])
    if len(left) == 3:
        low = low + (mul(left[1], right[1]) + (mul(left[0], right[2]) + mul(left[2], right[0])))
    return mul(left[0], right[0]) + low


def gather_kernel(chunks, order, ens, *outs):
    workers, per_chunk, rows, _ = outs[0].shape
    patches = ens.shape[0] // rows
    per_worker = per_chunk * chunks

    def one(worker, carry):
        for slot in range(per_worker):
            patch = order[worker * per_worker + slot]
            outs[slot // per_chunk][worker, slot % per_chunk] = ens[pl.ds(patch, rows, stride=patches), :]
        return carry

    lax.fori_loop(0, workers, one, 0)


def scatter_kernel(chunks, order, *refs):
    ins, out = refs[:-1], refs[-1]
    workers, per_chunk, rows, _ = ins[0].shape
    patches = out.shape[0] // rows
    per_worker = per_chunk * chunks

    def one(worker, carry):
        for slot in range(per_worker):
            patch = order[worker * per_worker + slot]
            out[pl.ds(patch, rows, stride=patches), :] = ins[slot // per_chunk][worker, slot % per_chunk]
        return carry

    lax.fori_loop(0, workers, one, 0)


def slots_kernel(count, index, values, precision, out):
    patches, slots = index.shape
    channels = out.shape[2]
    place = lax.broadcasted_iota(jnp.int32, (channels, slots), 0)
    lane = lax.broadcasted_iota(jnp.int32, (1, slots), 1)
    for p in range(patches):
        weight = jnp.where(lane < count[0, p], precision[p : p + 1, :], 0.0)
        rows = split(weight, 3) + split(weight * values[p : p + 1, :], 3)
        rows = jnp.concatenate([row.astype(F) for row in rows] + [jnp.zeros((2, slots), F)], axis=0).astype(BF)
        picker = jnp.where(place == index[p : p + 1, :], 1.0, 0.0).astype(BF)
        sums = dot_t(rows, picker)
        total = sums[0:1] + (sums[1:2] + sums[2:3])
        valued = sums[3:4] + (sums[4:5] + sums[5:6])
        out[p] = jnp.concatenate([total, jnp.sqrt(total), valued, jnp.zeros((5, channels), F)], axis=0)


def double_poly(mats, pieces):
    parts = [split(m, pieces) for m in mats]
    squares = [product(p[:2], p[:2]) for p in parts]
    outer = [split(s, 2) for s in squares]
    inner = [split(0.0625 * s - 0.5625 * m, 2) for s, m in zip(squares, mats)]
    poly = [
        product(o, i) + (1.6875 * s - 2.4375 * m) for o, i, s, m in zip(outer, inner, squares, mats)
    ]
    return parts, poly


def double_step(mats, roots, pieces):
    parts, poly = double_poly(mats, pieces)
    spoly = [split(p, pieces) for p in poly]
    if roots is None:
        size = mats[0].shape[0]
        row = lax.broadcasted_iota(jnp.int32, (size, size), 0)
        col = lax.broadcasted_iota(jnp.int32, (size, size), 1)
        new_roots = [jnp.where(row == col, p + 2.25, p) for p in poly]
    else:
        new_roots = [2.25 * z + product(split(z, 2), p[:2]) for z, p in zip(roots, spoly)]
    half = [2.25 * m + product(s, p) for m, s, p in zip(mats, parts, spoly)]
    new_mats = [2.25 * u + product(split(u, pieces), p) for u, p in zip(half, spoly)]
    return new_mats, new_roots


def analyse_kernel(members, doubles, state, sums, operator, *refs):
    transform, updated = refs[-2:]
    n = transform.shape[0]
    cells = state.shape[3]
    every = range(n)
    row = lax.broadcasted_iota(jnp.int32, (members, members), 0)
    col = lax.broadcasted_iota(jnp.int32, (members, members), 1)
    inflation = members - 1.0

    oper = split(operator[...], 3)
    mats, traces, projected = [], [], []
    states = [state[:, i].reshape(members, cells) for i in every]
    mapped = [product(split(x, 3), oper) for x in states]
    for i in every:
        mean = jnp.mean(mapped[i], axis=0, keepdims=True)
        pert = mapped[i] - mean
        innov = sums[i, 2:3] - mean * sums[i, 0:1]
        projected.append(jnp.sum(pert * innov, axis=1, keepdims=True))
        scaled = pert * sums[i, 1:2]
        trace = jnp.sum(jnp.sum(scaled * scaled, axis=0, keepdims=True), axis=1, keepdims=True)
        traces.append(trace + inflation * members)
        mats.append(scaled)
    pieces = [split(m, 3) for m in mats]
    grams = [product(p, p, dot_t) for p in pieces]
    mats = [jnp.where(row == col, g + inflation, g) / t for g, t in zip(grams, traces)]

    mats, roots = double_step(mats, None, 3)
    mats, roots = lax.fori_loop(0, doubles - 2, lambda k, c: double_step(c[0], c[1], 2), (mats, roots))
    _, poly = double_poly(mats, 2)
    roots = [2.25 * z + product(split(z, 2), split(p, 2)) for z, p in zip(roots, poly)]

    for i in every:
        root, trace = roots[i], traces[i]
        scale = math.sqrt(inflation) / jnp.sqrt(trace)
        transform[i] = root * scale
        x = state[:, i].reshape(members, cells)
        mean = jnp.mean(x, axis=0, keepdims=True)
        pert = x - mean
        once = jnp.sum(root * projected[i], axis=0, keepdims=True)
        weight = jnp.sum(root * once, axis=1, keepdims=True) / trace
        shift = mean + jnp.sum(pert * weight, axis=0, keepdims=True)
        result = shift + scale * product(split(root, 2), split(pert, 2))
        updated[:, i] = result.reshape(updated.shape[0], updated.shape[2], cells)


def analyse(chunk, chunks, state, sums, operator, transform):
    workers, per_chunk, rows, cells = state.shape
    members = workers * rows
    channels = sums.shape[2]
    n = min(LOCKSTEP, per_chunk)
    steps = per_chunk // n
    first = chunk * steps
    in_specs = [
        pl.BlockSpec((workers, n, rows, cells), lambda i: (0, i, 0, 0)),
        pl.BlockSpec((n, 8, channels), lambda i: (first + i, 0, 0)),
        pl.BlockSpec((cells, channels), lambda i: (0, 0)),
    ]
    args = [state, sums, operator]
    aliases = {}
    if transform is not None:
        in_specs.append(pl.BlockSpec(memory_space=pl.ANY))
        args.append(transform)
        aliases = {3: 0}
    return pl.pallas_call(
        functools.partial(analyse_kernel, members, 6),
        grid=(steps,),
        in_specs=in_specs,
        out_specs=[
            pl.BlockSpec((n, members, members), lambda i: (first + i, 0, 0)),
            pl.BlockSpec((workers, n, rows, cells), lambda i: (0, i, 0, 0)),
        ],
        out_shape=[
            jax.ShapeDtypeStruct((per_chunk * chunks, members, members), F),
            jax.ShapeDtypeStruct(state.shape, F),
        ],
        input_output_aliases=aliases,
        compiler_params=pltpu.CompilerParams(vmem_limit_bytes=VMEM),
        cost_estimate=pl.CostEstimate(
            flops=per_chunk * 100 * 2 * members**3, bytes_accessed=12 * per_chunk * members**2, transcendentals=0
        ),
        name="analyse",
    )(*args)


def local(ensemble, column_operator, patch_order, obs_index, obs_count, obs_values, obs_precision):
    rows, band_patches, cells = ensemble.shape
    workers = lax.axis_size("mem")
    worker = lax.axis_index("mem")
    per_worker = band_patches // workers
    per_chunk = per_worker // CHUNKS
    levels = column_operator.shape[0]
    columns = cells // levels
    channels = columns * column_operator.shape[1]
    smem = pl.BlockSpec(memory_space=pltpu.SMEM)
    vmem = pl.BlockSpec(memory_space=pltpu.VMEM)
    params = pltpu.CompilerParams(vmem_limit_bytes=VMEM)
    piece = jax.ShapeDtypeStruct((workers, per_chunk, rows, cells), F)
    order = patch_order[0]
    lanes = cells // LANES
    strip = pl.BlockSpec((rows * band_patches, LANES), lambda j: (0, j))
    block = pl.BlockSpec((workers, per_chunk, rows, LANES), lambda j: (0, 0, 0, j))

    listed = pl.pallas_call(
        functools.partial(gather_kernel, CHUNKS),
        grid=(lanes,),
        in_specs=[smem, strip],
        out_specs=[block] * CHUNKS,
        out_shape=[piece] * CHUNKS,
        compiler_params=params,
        name="gather",
    )(order, ensemble.reshape(rows * band_patches, cells))

    my_index = lax.dynamic_slice_in_dim(obs_index[0], worker * per_worker, per_worker, 0)
    sums = pl.pallas_call(
        slots_kernel,
        in_specs=[smem, vmem, vmem, vmem],
        out_specs=vmem,
        out_shape=jax.ShapeDtypeStruct((per_worker, 8, channels), F),
        compiler_params=params,
        name="slots",
    )(obs_count, my_index, obs_values[0], obs_precision[0])
    width = column_operator.shape[1]
    operator = jnp.concatenate(
        [jnp.pad(column_operator, ((0, 0), (k * width, channels - (k + 1) * width))) for k in range(columns)]
    )

    transform = None
    returned = []
    states = [lax.all_to_all(x, "mem", 0, 0, tiled=True) for x in listed]
    for c in range(CHUNKS):
        transform, updated = analyse(c, CHUNKS, states[c], sums, operator, transform)
        returned.append(lax.all_to_all(updated, "mem", 0, 0, tiled=True))

    restored = pl.pallas_call(
        functools.partial(scatter_kernel, CHUNKS),
        grid=(lanes,),
        in_specs=[smem] + [block] * CHUNKS,
        out_specs=strip,
        out_shape=jax.ShapeDtypeStruct((rows * band_patches, cells), F),
        compiler_params=params,
        name="scatter",
    )(order, *returned)
    return (restored.reshape(rows, band_patches, cells), transform[None])


def solution(mesh):
    placed = (
        P("mem", "band", None),
        P(),
        P("band", None),
        P("band", None, None),
        P("band", "mem"),
        P("band", "mem", None),
        P("band", "mem", None),
    )
    return jax.shard_map(
        local,
        mesh=mesh,
        in_specs=placed,
        out_specs=(P("mem", "band", None), P("band", "mem", None, None)),
        check_vma=False,
    )
```

time: 294 us -> 121 us (0.41)
  matrix products: 161 us -> 0 us
  local copies, waits for them, and re-layouts: 51 us -> 1.94 us
  Pallas kernels: 0 us -> 47.9 us
  blocking collectives: 0 us -> 35.3 us
  waiting for transfers between devices: 51.7 us -> 24.4 us
  other arithmetic: 10.7 us -> 0.72 us
  starting transfers between devices: 16.5 us -> 9.73 us
    dot_general x45 -> x0, matrix products: 161 us -> none  [the longest x36 128 us: batched(): jnp.einsum('pij,pjk->pik', left, right, precision=lax.Precision.HIGHEST)]
    pallas_call x0 -> x4, Pallas kernels: none -> 47.9 us  [the longest x1 37.1 us: analyse(): pl.pallas_call(functools.partial(analyse_kernel, members, 6), grid=(steps...]
    all_to_all x0 -> x1, blocking collectives: none -> 35.3 us  [local(): returned.append(lax.all_to_all(updated, 'mem', 0, 0, tiled=True))]
    while x48 -> x0, local copies, waits for them, and re-layouts: 29.3 us -> none
    all_to_all x2 -> x1, waiting for transfers between devices: 51.7 us -> 24.4 us  [local(): states = [lax.all_to_all(x, 'mem', 0, 0, tiled=True) for x in listed]]
    all_to_all x2 -> x1, starting transfers between devices: 16.5 us -> 9.73 us  [local(): states = [lax.all_to_all(x, 'mem', 0, 0, tiled=True) for x in listed]]
    reshape x2 -> x0, local copies, waits for them, and re-layouts: 5.53 us -> none  [the longest x1 2.89 us: map_columns(): return mapped.reshape(rows, patches, -1)]
    all_to_all x1 -> x0, local copies, waits for them, and re-layouts: 3.78 us -> none  [local(): lax.all_to_all(listed, 'mem', split_axis=1, concat_axis=0, tiled=True)]
  transfers between devices with their start and end apart: 2 -> 1, of which waited for: 2 -> 1; matrix products, arithmetic and copies ran while one was open for 1% -> 1% of each run, Pallas kernels for 0% -> 2%
where the time goes in v1:
time: 121 us
  Pallas kernels  47.9 us (40%)
  blocking collectives  35.3 us (29%)
  waiting for transfers between devices  24.4 us (20%)
  starting transfers between devices  9.73 us (8%)
  local copies, waits for them, and re-layouts  1.94 us (2%)
    pallas_call x1, Pallas kernels, analyse(): pl.pallas_call(functools.partial(analyse_kernel, members, 6), grid=(steps...  37.1 us
    all_to_all x1, blocking collectives, local(): returned.append(lax.all_to_all(updated, 'mem', 0, 0, tiled=True))  35.3 us
    all_to_all x1, waiting for transfers between devices, local(): states = [lax.all_to_all(x, 'mem', 0, 0, tiled=True) for x in listed]  24.4 us
    all_to_all x1, starting transfers between devices, local(): states = [lax.all_to_all(x, 'mem', 0, 0, tiled=True) for x in listed]  9.73 us
    pallas_call x1, Pallas kernels, local(): pl.pallas_call(functools.partial(gather_kernel, CHUNKS), grid=(lanes,), i...  4.96 us
    pallas_call x1, Pallas kernels, local(): pl.pallas_call(functools.partial(scatter_kernel, CHUNKS), grid=(lanes,),...  3.75 us
  transfers between devices with their start and end apart: 1, of which 1 were waited for; matrix products, arithmetic and copies ran while one was open for 1% of the time, Pallas kernels for 2%

profile of v1, /device:TPU:1, one launch (start us, length us, event | category | flops | bytes accessed | tf_op | source)
XLA Modules:
  0.0 120.6 jit_solution(5064053885493561726)
XLA Ops:
  0.6 0.0 copy-start
  0.6 5.0 %gather.1 = f32[32,8,8,256]{3,2,1,0:T(8,128)} custom-call(s32[256]{0:T(256)} %bitcast.12, f32[2048,256]{1,0:T(8,128)} %bitcast.8), custom_call_target="tpu_custom_call" | custom-call | tf_op jit(solution)/shard_map/gather/pallas_call | solution.py:216
  5.6 0.0 copy-start.2
  5.6 9.7 %all-to-all-start = ((f32[32,8,8,256]{3,2,1,0:T(8,128)}), f32[32,8,8,256]{3,2,1,0:T(8,128)S(1)}, u32[]{:S(2)}, u32[]{:S(2)}) async-start(f32[32,8,8,256]{3,2,1,0:T(8,128)} %gather.1), calls=%async_computation | async-start | bytes 4194304 | tf_op jit(solution)/shard_map/all_to_all | solution.py:242
  15.4 0.0 copy-done
  15.4 0.6 dynamic-slice_bitcast_fusion.index
  16.0 2.1 %slots.1.sums = f32[8,8,256]{2,1,0:T(8,128)} custom-call(s32[1,8]{1,0:T(1,128)} %count.1, s32[8,512]{1,0:T(8,128)} %dynamic-slice_bitcast_fusion.index, f32[8,512]{1,0:T(8,128)} %bitcast.10, f32[8,512]{1,0:T(8,128)} %bitcast.11), custom_call_target="tpu_custom_call" | custom-call | tf_op jit(solution)/shard_map/slots/pallas_call | solution.py:227
  18.1 0.0 copy-done.2
  18.1 0.7 select_maximum_fusion.operator
  18.8 24.4 %all-to-all-done.state = f32[32,8,8,256]{3,2,1,0:T(8,128)S(1)} async-done(((f32[32,8,8,256]{3,2,1,0:T(8,128)}), f32[32,8,8,256]{3,2,1,0:T(8,128)S(1)}, u32[]{:S(2)}, u32[]{:S(2)}) %all-to-all-start) | async-done | bytes 2097184 | tf_op jit(solution)/shard_map/all_to_all | solution.py:242
  43.2 0.0 copy-start.1
  43.2 1.3 %copy-done.1 = f32[32,8,8,256]{3,2,1,0:T(8,128)} copy-done((f32[32,8,8,256]{3,2,1,0:T(8,128)}, f32[32,8,8,256]{3,2,1,0:T(8,128)S(1)}, u32[]{:S(2)}) %copy-start.1) | copy-done | bytes 2097176
  44.5 37.1 %analyse.1 = (f32[8,256,256]{2,1,0:T(8,128)}, f32[32,8,8,256]{3,2,1,0:T(8,128)}) custom-call(f32[32,8,8,256]{3,2,1,0:T(8,128)} %copy-done.1, f32[8,8,256]{2,1,0:T(8,128)} %slots.1.sums, f32[256,256]{1,0:T(8,128)} %select_maximum_fusion.operator), custom_call_target="tpu_custom_call" | custom-call | flops 26843545600 | bytes 6291456 | tf_op jit(solution)/shard_map/analyse/pallas_call | solution.py:177
  81.6 35.3 %all_to_all.10.refs_0_ = f32[32,8,8,256]{3,2,1,0:T(8,128)} all-to-all(f32[32,8,8,256]{3,2,1,0:T(8,128)} %get-tuple-element.4), channel_id=1, replica_groups=mesh['mem'=32,'band'=4] {'mem'}, dimensions={0} | all-to-all | bytes 4194304 | tf_op jit(solution)/shard_map/all_to_all | solution.py:245
  116.9 3.8 %scatter.1 = f32[2048,256]{1,0:T(8,128)} custom-call(s32[256]{0:T(256)} %bitcast.13, f32[32,8,8,256]{3,2,1,0:T(8,128)} %all_to_all.10.refs_0_), custom_call_target="tpu_custom_call" | custom-call | tf_op jit(solution)/shard_map/scatter/pallas_call | solution.py:247
Async XLA Ops:
  0.6 14.7 %copy-start = (s32[1,256,512]{2,1,0:T(8,128)S(1)}, s32[1,256,512]{2,1,0:T(8,128)}, u32[]{:S(2)}) copy-start(s32[1,256,512]{2,1,0:T(8,128)} %param.10) | copy-start | bytes 1572868
  5.6 12.5 %copy-start.2 = (f32[128,128]{1,0:T(8,128)S(1)}, f32[128,128]{1,0:T(8,128)}, u32[]{:S(2)}) copy-start(f32[128,128]{1,0:T(8,128)} %param.8) | copy-start | bytes 196612
  5.6 37.6 %all-to-all-start = ((f32[32,8,8,256]{3,2,1,0:T(8,128)}), f32[32,8,8,256]{3,2,1,0:T(8,128)S(1)}, u32[]{:S(2)}, u32[]{:S(2)}) async-start(f32[32,8,8,256]{3,2,1,0:T(8,128)} %gather.1), calls=%async_computation | async-start | bytes 4194304 | tf_op jit(solution)/shard_map/all_to_all | solution.py:242
  43.2 1.3 %copy-start.1 = (f32[32,8,8,256]{3,2,1,0:T(8,128)}, f32[32,8,8,256]{3,2,1,0:T(8,128)S(1)}, u32[]{:S(2)}) copy-start(f32[32,8,8,256]{3,2,1,0:T(8,128)S(1)} %all-to-all-done.state) | copy-start | bytes 6291460

commit v2 on v1

--- a/solution.py
+++ b/solution.py
@@ -10,7 +10,7 @@
 
 F = jnp.float32
 BF = jnp.bfloat16
-CHUNKS = 1
+CHUNKS = 2
 LOCKSTEP = 4
 LANES = 128
 VMEM = 56 * 2**20
@@ -34,21 +34,30 @@
 
 
 def product(left, right, mul=dot):
-    low = mul(left[0], right[1]) + mul(left[1], right[0])
-    if len(left) == 3:
-        low = low + (mul(left[1], right[1]) + (mul(left[0], right[2]) + mul(left[2], right[0])))
-    return mul(left[0], right[0]) + low
-
-
-def gather_kernel(chunks, order, ens, *outs):
-    workers, per_chunk, rows, _ = outs[0].shape
+    n = left[0].shape[0]
+    first = mul(jnp.concatenate(left, axis=0), right[0])
+    if len(left) == 2:
+        return first[:n] + (first[n:] + mul(left[0], right[1]))
+    second = mul(jnp.concatenate(left[:2], axis=0), right[1])
+    low = second[n:] + (mul(left[0], right[2]) + first[2 * n :])
+    return first[:n] + ((first[n : 2 * n] + second[:n]) + low)
+
+
+def stacked(left, other, right):
+    both = [jnp.concatenate([a, b], axis=0) for a, b in zip(left, other)]
+    result = product(both, right)
+    n = left[0].shape[0]
+    return result[:n], result[n:]
+
+
+def gather_kernel(chunk, per_worker, order, ens, out):
+    workers, per_chunk, rows, _ = out.shape
     patches = ens.shape[0] // rows
-    per_worker = per_chunk * chunks
 
     def one(worker, carry):
-        for slot in range(per_worker):
-            patch = order[worker * per_worker + slot]
-            outs[slot // per_chunk][worker, slot % per_chunk] = ens[pl.ds(patch, rows, stride=patches), :]
+        for slot in range(per_chunk):
+            patch = order[worker * per_worker + chunk * per_chunk + slot]
+            out[worker, slot] = ens[pl.ds(patch, rows, stride=patches), :]
         return carry
 
     lax.fori_loop(0, workers, one, 0)
@@ -104,9 +113,13 @@
         row = lax.broadcasted_iota(jnp.int32, (size, size), 0)
         col = lax.broadcasted_iota(jnp.int32, (size, size), 1)
         new_roots = [jnp.where(row == col, p + 2.25, p) for p in poly]
+        half = [2.25 * m + product(s, p) for m, s, p in zip(mats, parts, spoly)]
     else:
-        new_roots = [2.25 * z + product(split(z, 2), p[:2]) for z, p in zip(roots, spoly)]
-    half = [2.25 * m + product(s, p) for m, s, p in zip(mats, parts, spoly)]
+        half, new_roots = [], []
+        for m, z, s, p in zip(mats, roots, parts, spoly):
+            upper, lower = stacked(s, split(z, 2), p)
+            half.append(2.25 * m + upper)
+            new_roots.append(2.25 * z + lower)
     new_mats = [2.25 * u + product(split(u, pieces), p) for u, p in zip(half, spoly)]
     return new_mats, new_roots
 
@@ -138,7 +151,8 @@
     mats = [jnp.where(row == col, g + inflation, g) / t for g, t in zip(grams, traces)]
 
     mats, roots = double_step(mats, None, 3)
-    mats, roots = lax.fori_loop(0, doubles - 2, lambda k, c: double_step(c[0], c[1], 2), (mats, roots))
+    for _ in range(doubles - 2):
+        mats, roots = double_step(mats, roots, 2)
     _, poly = double_poly(mats, 2)
     roots = [2.25 * z + product(split(z, 2), split(p, 2)) for z, p in zip(roots, poly)]
 
@@ -213,15 +227,19 @@
     strip = pl.BlockSpec((rows * band_patches, LANES), lambda j: (0, j))
     block = pl.BlockSpec((workers, per_chunk, rows, LANES), lambda j: (0, 0, 0, j))
 
-    listed = pl.pallas_call(
-        functools.partial(gather_kernel, CHUNKS),
-        grid=(lanes,),
-        in_specs=[smem, strip],
-        out_specs=[block] * CHUNKS,
-        out_shape=[piece] * CHUNKS,
-        compiler_params=params,
-        name="gather",
-    )(order, ensemble.reshape(rows * band_patches, cells))
+    listed = [
+        pl.pallas_call(
+            functools.partial(gather_kernel, c, per_worker),
+            grid=(lanes,),
+            in_specs=[smem, strip],
+            out_specs=block,
+            out_shape=piece,
+            compiler_params=params,
+            cost_estimate=pl.CostEstimate(flops=0, bytes_accessed=2 * ensemble.size * 4, transcendentals=0),
+            name="gather",
+        )(order, ensemble.reshape(rows * band_patches, cells))
+        for c in range(CHUNKS)
+    ]
 
     my_index = lax.dynamic_slice_in_dim(obs_index[0], worker * per_worker, per_worker, 0)
     sums = pl.pallas_call(

time: 121 us -> 108 us (0.89)
  waiting for transfers between devices: 24.4 us -> 10 us
  starting transfers between devices: 9.73 us -> 21.1 us
  blocking collectives: 35.3 us -> 24.7 us
  local copies, waits for them, and re-layouts: 1.94 us -> 0.63 us
    all_to_all x1 -> x2, waiting for transfers between devices: 24.4 us -> 10 us  [local(): states = [lax.all_to_all(x, 'mem', 0, 0, tiled=True) for x in listed]]
    all_to_all x1, blocking collectives: 35.3 us -> 24.7 us  [local(): returned.append(lax.all_to_all(updated, 'mem', 0, 0, tiled=True))]
    all_to_all x0 -> x1, starting transfers between devices: none -> 7.49 us  [local(): returned.append(lax.all_to_all(updated, 'mem', 0, 0, tiled=True))]
    all_to_all x1 -> x2, starting transfers between devices: 9.73 us -> 13.6 us  [local(): states = [lax.all_to_all(x, 'mem', 0, 0, tiled=True) for x in listed]]
    pallas_call x1 -> x2, Pallas kernels: 4.96 us -> 7.39 us  [local(): pl.pallas_call(functools.partial(gather_kernel, c, per_worker), grid=(lan...]
    unnamed x6 -> x10, local copies, waits for them, and re-layouts: 1.33 us -> 0.03 us
    pallas_call x1 -> x2, Pallas kernels: 37.1 us -> 35.8 us  [analyse(): pl.pallas_call(functools.partial(analyse_kernel, members, 6), grid=(steps...]
  transfers between devices with their start and end apart: 1 -> 3, of which waited for: 1 -> 1; matrix products, arithmetic and copies ran while one was open for 1% -> 1% of each run, Pallas kernels for 2% -> 39%
where the time goes in v2:
time: 108 us; the launch traced here: 107 us
  Pallas kernels  49.1 us (45%)
  blocking collectives  24.7 us (23%)
  starting transfers between devices  21.1 us (20%)
  waiting for transfers between devices  10 us (9%)
    pallas_call x2, Pallas kernels, analyse(): pl.pallas_call(functools.partial(analyse_kernel, members, 6), grid=(steps...  35.8 us
    all_to_all x1, blocking collectives, local(): returned.append(lax.all_to_all(updated, 'mem', 0, 0, tiled=True))  24.7 us
    all_to_all x2, starting transfers between devices, local(): states = [lax.all_to_all(x, 'mem', 0, 0, tiled=True) for x in listed]  13.6 us
    all_to_all x2, waiting for transfers between devices, local(): states = [lax.all_to_all(x, 'mem', 0, 0, tiled=True) for x in listed]  10 us
    all_to_all x1, starting transfers between devices, local(): returned.append(lax.all_to_all(updated, 'mem', 0, 0, tiled=True))  7.49 us
    pallas_call x2, Pallas kernels, local(): pl.pallas_call(functools.partial(gather_kernel, c, per_worker), grid=(lan...  7.39 us
    pallas_call x1, Pallas kernels, local(): pl.pallas_call(functools.partial(scatter_kernel, CHUNKS), grid=(lanes,),...  3.7 us
  transfers between devices with their start and end apart: 3, of which 1 were waited for; matrix products, arithmetic and copies ran while one was open for 1% of the time, Pallas kernels for 39%

profile of v2, /device:TPU:1, one launch (start us, length us, event | category | flops | bytes accessed | tf_op | source)
XLA Modules:
  0.0 106.8 jit_solution(18092124553560467921)
XLA Ops:
  0.6 0.0 copy-start
  0.6 3.7 %gather.2 = f32[32,4,8,256]{3,2,1,0:T(8,128)} custom-call(s32[256]{0:T(256)} %bitcast.13, f32[2048,256]{1,0:T(8,128)} %bitcast.8), custom_call_target="tpu_custom_call" | custom-call | bytes 4194304 | tf_op jit(solution)/shard_map/gather/pallas_call | solution.py:231
  4.3 9.6 %all-to-all-start = ((f32[32,4,8,256]{3,2,1,0:T(8,128)}), f32[32,4,8,256]{3,2,1,0:T(8,128)S(1)}, u32[]{:S(2)}, u32[]{:S(2)}) async-start(f32[32,4,8,256]{3,2,1,0:T(8,128)} %gather.2), calls=%async_computation | async-start | bytes 2097152 | tf_op jit(solution)/shard_map/all_to_all | solution.py:260
  13.9 0.0 copy-start.4
  13.9 3.7 %gather.3 = f32[32,4,8,256]{3,2,1,0:T(8,128)} custom-call(s32[256]{0:T(256)} %bitcast.14, f32[2048,256]{1,0:T(8,128)} %bitcast.9), custom_call_target="tpu_custom_call" | custom-call | bytes 4194304 | tf_op jit(solution)/shard_map/gather/pallas_call | solution.py:231
  17.7 0.0 copy-done
  17.7 0.6 dynamic-slice_bitcast_fusion.index
  18.3 2.1 %slots.1.sums = f32[8,8,256]{2,1,0:T(8,128)} custom-call(s32[1,8]{1,0:T(1,128)} %count.1, s32[8,512]{1,0:T(8,128)} %dynamic-slice_bitcast_fusion.index, f32[8,512]{1,0:T(8,128)} %bitcast.11, f32[8,512]{1,0:T(8,128)} %bitcast.12), custom_call_target="tpu_custom_call" | custom-call | tf_op jit(solution)/shard_map/slots/pallas_call | solution.py:245
  20.4 0.0 copy-done.4
  20.4 0.7 select_maximum_fusion.operator
  21.1 10.0 %all-to-all-done.state = f32[32,4,8,256]{3,2,1,0:T(8,128)S(1)} async-done(((f32[32,4,8,256]{3,2,1,0:T(8,128)}), f32[32,4,8,256]{3,2,1,0:T(8,128)S(1)}, u32[]{:S(2)}, u32[]{:S(2)}) %all-to-all-start) | async-done | bytes 1048608 | tf_op jit(solution)/shard_map/all_to_all | solution.py:260
  31.1 0.0 copy-start.2
  31.1 4.0 %all-to-all-start.2 = ((f32[32,4,8,256]{3,2,1,0:T(8,128)}), f32[32,4,8,256]{3,2,1,0:T(8,128)S(1)}, u32[]{:S(2)}, u32[]{:S(2)}) async-start(f32[32,4,8,256]{3,2,1,0:T(8,128)} %gather.3), calls=%async_computation.2 | async-start | bytes 2097152 | tf_op jit(solution)/shard_map/all_to_all | solution.py:260
  35.1 0.0 copy-done.2
  35.1 17.9 %analyse.2 = (f32[8,256,256]{2,1,0:T(8,128)}, f32[32,4,8,256]{3,2,1,0:T(8,128)}) custom-call(f32[32,4,8,256]{3,2,1,0:T(8,128)} %copy-done.2, f32[8,8,256]{2,1,0:T(8,128)} %slots.1.sums, f32[256,256]{1,0:T(8,128)} %select_maximum_fusion.operator), custom_call_target="tpu_custom_call" | custom-call | flops 13421772800 | bytes 3145728 | tf_op jit(solution)/shard_map/analyse/pallas_call | solution.py:191
  53.0 0.0 all-to-all-done.2.state
  53.0 0.0 copy-start.3
  53.0 7.5 %all-to-all-start.1 = ((f32[32,4,8,256]{3,2,1,0:T(8,128)}), f32[32,4,8,256]{3,2,1,0:T(8,128)S(1)}, u32[]{:S(2)}, u32[]{:S(2)}) async-start(f32[32,4,8,256]{3,2,1,0:T(8,128)} %get-tuple-element.6), calls=%async_computation.1 | async-start | bytes 2097152 | tf_op jit(solution)/shard_map/all_to_all | solution.py:263
  60.5 0.0 copy-done.3
  60.5 17.9 %analyse.3 = (f32[8,256,256]{2,1,0:T(8,128)}, f32[32,4,8,256]{3,2,1,0:T(8,128)}) custom-call(f32[32,4,8,256]{3,2,1,0:T(8,128)} %copy-done.3, f32[8,8,256]{2,1,0:T(8,128)} %slots.1.sums, f32[256,256]{1,0:T(8,128)} %select_maximum_fusion.operator, f32[8,256,256]{2,1,0:T(8,128)} %get-tuple-element.7.refs_0_), custom_call_target="tpu_custom_call", output_to_operand_aliasing={{0}: (3, {})} | custom-call | flops 13421772800 | bytes 3145728 | tf_op jit(solution)/shard_map/analyse/pallas_call | solution.py:191
  78.5 0.0 all-to-all-done.1.refs_0_
  78.5 0.0 copy-start.1
  78.5 24.7 %all_to_all.20.refs_1_ = f32[32,4,8,256]{3,2,1,0:T(8,128)} all-to-all(f32[32,4,8,256]{3,2,1,0:T(8,128)} %get-tuple-element.8), channel_id=1, replica_groups=mesh['mem'=32,'band'=4] {'mem'}, dimensions={0} | all-to-all | bytes 2097152 | tf_op jit(solution)/shard_map/all_to_all | solution.py:263
  103.1 0.0 copy-done.1
  103.1 3.7 %scatter.1 = f32[2048,256]{1,0:T(8,128)} custom-call(s32[256]{0:T(256)} %bitcast.15, f32[32,4,8,256]{3,2,1,0:T(8,128)} %copy-done.1, f32[32,4,8,256]{3,2,1,0:T(8,128)} %all_to_all.20.refs_1_), custom_call_target="tpu_custom_call" | custom-call | tf_op jit(solution)/shard_map/scatter/pallas_call | solution.py:265
Async XLA Ops:
  0.6 17.0 %copy-start = (s32[1,256,512]{2,1,0:T(8,128)S(1)}, s32[1,256,512]{2,1,0:T(8,128)}, u32[]{:S(2)}) copy-start(s32[1,256,512]{2,1,0:T(8,128)} %param.10) | copy-start | bytes 1572868
  4.3 26.8 %all-to-all-start = ((f32[32,4,8,256]{3,2,1,0:T(8,128)}), f32[32,4,8,256]{3,2,1,0:T(8,128)S(1)}, u32[]{:S(2)}, u32[]{:S(2)}) async-start(f32[32,4,8,256]{3,2,1,0:T(8,128)} %gather.2), calls=%async_computation | async-start | bytes 2097152 | tf_op jit(solution)/shard_map/all_to_all | solution.py:260
  13.9 6.5 %copy-start.4 = (f32[128,128]{1,0:T(8,128)S(1)}, f32[128,128]{1,0:T(8,128)}, u32[]{:S(2)}) copy-start(f32[128,128]{1,0:T(8,128)} %param.8) | copy-start | bytes 196612
  31.1 4.0 %copy-start.2 = (f32[32,4,8,256]{3,2,1,0:T(8,128)}, f32[32,4,8,256]{3,2,1,0:T(8,128)S(1)}, u32[]{:S(2)}) copy-start(f32[32,4,8,256]{3,2,1,0:T(8,128)S(1)} %all-to-all-done.state) | copy-start | bytes 3145732
  31.1 21.9 %all-to-all-start.2 = ((f32[32,4,8,256]{3,2,1,0:T(8,128)}), f32[32,4,8,256]{3,2,1,0:T(8,128)S(1)}, u32[]{:S(2)}, u32[]{:S(2)}) async-start(f32[32,4,8,256]{3,2,1,0:T(8,128)} %gather.3), calls=%async_computation.2 | async-start | bytes 2097152 | tf_op jit(solution)/shard_map/all_to_all | solution.py:260
  53.0 7.5 %copy-start.3 = (f32[32,4,8,256]{3,2,1,0:T(8,128)}, f32[32,4,8,256]{3,2,1,0:T(8,128)S(1)}, u32[]{:S(2)}) copy-start(f32[32,4,8,256]{3,2,1,0:T(8,128)S(1)} %all-to-all-done.2.state) | copy-start | bytes 3145732
  53.0 25.4 %all-to-all-start.1 = ((f32[32,4,8,256]{3,2,1,0:T(8,128)}), f32[32,4,8,256]{3,2,1,0:T(8,128)S(1)}, u32[]{:S(2)}, u32[]{:S(2)}) async-start(f32[32,4,8,256]{3,2,1,0:T(8,128)} %get-tuple-element.6), calls=%async_computation.1 | async-start | bytes 2097152 | tf_op jit(solution)/shard_map/all_to_all | solution.py:263
  78.5 24.7 %copy-start.1 = (f32[32,4,8,256]{3,2,1,0:T(8,128)}, f32[32,4,8,256]{3,2,1,0:T(8,128)S(1)}, u32[]{:S(2)}) copy-start(f32[32,4,8,256]{3,2,1,0:T(8,128)S(1)} %all-to-all-done.1.refs_0_) | copy-start | bytes 3145732

commit v3 on v2

--- a/solution.py
+++ b/solution.py
@@ -11,7 +11,7 @@
 F = jnp.float32
 BF = jnp.bfloat16
 CHUNKS = 2
-LOCKSTEP = 4
+ANALYSE_VMEM = 40 * 2**20
 LANES = 128
 VMEM = 56 * 2**20
 
@@ -60,7 +60,7 @@
             out[worker, slot] = ens[pl.ds(patch, rows, stride=patches), :]
         return carry
 
-    lax.fori_loop(0, workers, one, 0)
+    lax.fori_loop(0, workers, one, 0, unroll=4)
 
 
 def scatter_kernel(chunks, order, *refs):
@@ -75,7 +75,7 @@
             out[pl.ds(patch, rows, stride=patches), :] = ins[slot // per_chunk][worker, slot % per_chunk]
         return carry
 
-    lax.fori_loop(0, workers, one, 0)
+    lax.fori_loop(0, workers, one, 0, unroll=4)
 
 
 def slots_kernel(count, index, values, precision, out):
@@ -124,8 +124,8 @@
     return new_mats, new_roots
 
 
-def analyse_kernel(members, doubles, state, sums, operator, *refs):
-    transform, updated = refs[-2:]
+def analyse_kernel(members, doubles, first, state, sums, operator, *refs):
+    transform_out, updated, transform, leave = refs[-4:]
     n = transform.shape[0]
     cells = state.shape[3]
     every = range(n)
@@ -140,15 +140,15 @@
     for i in every:
         mean = jnp.mean(mapped[i], axis=0, keepdims=True)
         pert = mapped[i] - mean
-        innov = sums[i, 2:3] - mean * sums[i, 0:1]
+        innov = sums[first + i, 2:3] - mean * sums[first + i, 0:1]
         projected.append(jnp.sum(pert * innov, axis=1, keepdims=True))
-        scaled = pert * sums[i, 1:2]
+        scaled = pert * sums[first + i, 1:2]
         trace = jnp.sum(jnp.sum(scaled * scaled, axis=0, keepdims=True), axis=1, keepdims=True)
         traces.append(trace + inflation * members)
         mats.append(scaled)
     pieces = [split(m, 3) for m in mats]
     grams = [product(p, p, dot_t) for p in pieces]
-    mats = [jnp.where(row == col, g + inflation, g) / t for g, t in zip(grams, traces)]
+    mats = [jnp.where(row == col, g + inflation, g) * (1.0 / t) for g, t in zip(grams, traces)]
 
     mats, roots = double_step(mats, None, 3)
     for _ in range(doubles - 2):
@@ -168,40 +168,35 @@
         shift = mean + jnp.sum(pert * weight, axis=0, keepdims=True)
         result = shift + scale * product(split(root, 2), split(pert, 2))
         updated[:, i] = result.reshape(updated.shape[0], updated.shape[2], cells)
+    copy = pltpu.make_async_copy(transform, transform_out.at[pl.ds(first, n)], leave)
+    copy.start()
+    copy.wait()
 
 
 def analyse(chunk, chunks, state, sums, operator, transform):
     workers, per_chunk, rows, cells = state.shape
     members = workers * rows
-    channels = sums.shape[2]
-    n = min(LOCKSTEP, per_chunk)
-    steps = per_chunk // n
-    first = chunk * steps
-    in_specs = [
-        pl.BlockSpec((workers, n, rows, cells), lambda i: (0, i, 0, 0)),
-        pl.BlockSpec((n, 8, channels), lambda i: (first + i, 0, 0)),
-        pl.BlockSpec((cells, channels), lambda i: (0, 0)),
-    ]
-    args = [state, sums, operator]
+    anywhere = pl.BlockSpec(memory_space=pl.ANY)
+    vmem = pl.BlockSpec(memory_space=pltpu.VMEM)
+    first = chunk * per_chunk
+    in_specs = [vmem, vmem, vmem]
+    args = [pltpu.with_memory_space_constraint(state, pltpu.VMEM), sums, operator]
     aliases = {}
     if transform is not None:
-        in_specs.append(pl.BlockSpec(memory_space=pl.ANY))
+        in_specs.append(anywhere)
         args.append(transform)
         aliases = {3: 0}
     return pl.pallas_call(
-        functools.partial(analyse_kernel, members, 6),
-        grid=(steps,),
+        functools.partial(analyse_kernel, members, 6, first),
         in_specs=in_specs,
-        out_specs=[
-            pl.BlockSpec((n, members, members), lambda i: (first + i, 0, 0)),
-            pl.BlockSpec((workers, n, rows, cells), lambda i: (0, i, 0, 0)),
-        ],
+        out_specs=[anywhere, vmem],
         out_shape=[
             jax.ShapeDtypeStruct((per_chunk * chunks, members, members), F),
-            jax.ShapeDtypeStruct(state.shape, F),
+            pltpu.VMEM(state.shape, F),
         ],
+        scratch_shapes=[pltpu.VMEM((per_chunk, members, members), F), pltpu.SemaphoreType.DMA],
         input_output_aliases=aliases,
-        compiler_params=pltpu.CompilerParams(vmem_limit_bytes=VMEM),
+        compiler_params=pltpu.CompilerParams(vmem_limit_bytes=ANALYSE_VMEM),
         cost_estimate=pl.CostEstimate(
             flops=per_chunk * 100 * 2 * members**3, bytes_accessed=12 * per_chunk * members**2, transcendentals=0
         ),

time: 108 us -> 104 us (0.963)
  Pallas kernels: 49.1 us -> 44.5 us
  waiting for transfers between devices: 10 us -> 12.3 us
  blocking collectives: 24.7 us -> 23.4 us
    pallas_call x2, Pallas kernels: 35.8 us -> 32.3 us  [analyse(): pl.pallas_call(functools.partial(analyse_kernel, members, 6, first), in_s...]
    all_to_all x2, waiting for transfers between devices: 10 us -> 11.3 us  [local(): states = [lax.all_to_all(x, 'mem', 0, 0, tiled=True) for x in listed]]
    all_to_all x1, blocking collectives: 24.7 us -> 23.4 us  [local(): returned.append(lax.all_to_all(updated, 'mem', 0, 0, tiled=True))]
  transfers between devices with their start and end apart: 3 -> 3, of which waited for: 1 -> 3; matrix products, arithmetic and copies ran while one was open for 1% -> 1% of each run, Pallas kernels for 39% -> 36%
where the time goes in v3:
time: 104 us
  Pallas kernels  44.5 us (43%)
  blocking collectives  23.4 us (22%)
  starting transfers between devices  20.9 us (20%)
  waiting for transfers between devices  12.3 us (12%)
  local copies, waits for them, and re-layouts  1.58 us (2%)
    pallas_call x2, Pallas kernels, analyse(): pl.pallas_call(functools.partial(analyse_kernel, members, 6, first), in_s...  32.3 us
    all_to_all x1, blocking collectives, local(): returned.append(lax.all_to_all(updated, 'mem', 0, 0, tiled=True))  23.4 us
    all_to_all x2, starting transfers between devices, local(): states = [lax.all_to_all(x, 'mem', 0, 0, tiled=True) for x in listed]  13.6 us
    all_to_all x2, waiting for transfers between devices, local(): states = [lax.all_to_all(x, 'mem', 0, 0, tiled=True) for x in listed]  11.3 us
    all_to_all x1, starting transfers between devices, local(): returned.append(lax.all_to_all(updated, 'mem', 0, 0, tiled=True))  7.37 us
    pallas_call x2, Pallas kernels, local(): pl.pallas_call(functools.partial(gather_kernel, c, per_worker), grid=(lan...  6.64 us
    pallas_call x1, Pallas kernels, local(): pl.pallas_call(functools.partial(scatter_kernel, CHUNKS), grid=(lanes,),...  3.52 us
    pallas_call x1, Pallas kernels, local(): pl.pallas_call(slots_kernel, in_specs=[smem, vmem, vmem, vmem], out_specs...  2.12 us
  transfers between devices with their start and end apart: 3, of which 3 were waited for; matrix products, arithmetic and copies ran while one was open for 1% of the time, Pallas kernels for 36%

profile of v3, /device:TPU:1, one launch (start us, length us, event | category | flops | bytes accessed | tf_op | source)
XLA Modules:
  0.0 103.6 jit_solution(17134433338561953208)
XLA Ops:
  0.6 0.0 copy-start
  0.6 3.3 %gather.2 = f32[32,4,8,256]{3,2,1,0:T(8,128)} custom-call(s32[256]{0:T(256)} %bitcast.13, f32[2048,256]{1,0:T(8,128)} %bitcast.8), custom_call_target="tpu_custom_call" | custom-call | bytes 4194304 | tf_op jit(solution)/shard_map/gather/pallas_call | solution.py:226
  4.0 9.6 %all-to-all-start = ((f32[32,4,8,256]{3,2,1,0:T(8,128)}), f32[32,4,8,256]{3,2,1,0:T(8,128)S(1)}, u32[]{:S(2)}, u32[]{:S(2)}) async-start(f32[32,4,8,256]{3,2,1,0:T(8,128)} %gather.2), calls=%async_computation | async-start | bytes 2097152 | tf_op jit(solution)/shard_map/all_to_all | solution.py:255
  13.6 0.0 copy-start.3
  13.6 3.3 %gather.3 = f32[32,4,8,256]{3,2,1,0:T(8,128)} custom-call(s32[256]{0:T(256)} %bitcast.14, f32[2048,256]{1,0:T(8,128)} %bitcast.9), custom_call_target="tpu_custom_call" | custom-call | bytes 4194304 | tf_op jit(solution)/shard_map/gather/pallas_call | solution.py:226
  16.9 0.0 copy-done
  16.9 0.6 dynamic-slice_bitcast_fusion.index
  17.5 2.1 %slots.1.sums = f32[8,8,256]{2,1,0:T(8,128)} custom-call(s32[1,8]{1,0:T(1,128)} %count.1, s32[8,512]{1,0:T(8,128)} %dynamic-slice_bitcast_fusion.index, f32[8,512]{1,0:T(8,128)} %bitcast.11, f32[8,512]{1,0:T(8,128)} %bitcast.12), custom_call_target="tpu_custom_call" | custom-call | tf_op jit(solution)/shard_map/slots/pallas_call | solution.py:240
  19.6 0.0 copy-done.3
  19.6 0.0 copy-start.2
  19.7 11.1 %all-to-all-done.state = f32[32,4,8,256]{3,2,1,0:T(8,128)S(1)} async-done(((f32[32,4,8,256]{3,2,1,0:T(8,128)}), f32[32,4,8,256]{3,2,1,0:T(8,128)S(1)}, u32[]{:S(2)}, u32[]{:S(2)}) %all-to-all-start) | async-done | bytes 1048608 | tf_op jit(solution)/shard_map/all_to_all | solution.py:255
  30.7 4.0 %all-to-all-start.2 = ((f32[32,4,8,256]{3,2,1,0:T(8,128)}), f32[32,4,8,256]{3,2,1,0:T(8,128)S(1)}, u32[]{:S(2)}, u32[]{:S(2)}) async-start(f32[32,4,8,256]{3,2,1,0:T(8,128)} %gather.3), calls=%async_computation.2 | async-start | bytes 2097152 | tf_op jit(solution)/shard_map/all_to_all | solution.py:255
  34.7 0.0 copy-done.2
  34.7 16.1 %analyse.2 = (f32[8,256,256]{2,1,0:T(8,128)}, f32[32,4,8,256]{3,2,1,0:T(8,128)S(1)}) custom-call(f32[32,4,8,256]{3,2,1,0:T(8,128)S(1)} %all-to-all-done.state, f32[8,8,256]{2,1,0:T(8,128)S(1)} %copy-done.2, f32[256,256]{1,0:T(8,128)S(1)} %select_maximum_fusion.operator), custom_call_target="tpu_custom_call" | custom-call | flops 13421772800 | bytes 3145728 | tf_op jit(solution)/shard_map/analyse/pallas_call | solution.py:189
  50.9 0.0 copy-start.1
  50.9 1.0 copy-done.1
  51.8 0.2 all-to-all-done.2.state
  52.0 7.4 %all-to-all-start.1 = ((f32[32,4,8,256]{3,2,1,0:T(8,128)}), f32[32,4,8,256]{3,2,1,0:T(8,128)}, u32[]{:S(2)}, u32[]{:S(2)}) async-start(f32[32,4,8,256]{3,2,1,0:T(8,128)} %copy-done.1), calls=%async_computation.1 | async-start | bytes 2097152 | tf_op jit(solution)/shard_map/all_to_all | solution.py:258
  59.4 16.2 %analyse.3 = (f32[8,256,256]{2,1,0:T(8,128)}, f32[32,4,8,256]{3,2,1,0:T(8,128)S(1)}) custom-call(f32[32,4,8,256]{3,2,1,0:T(8,128)S(1)} %all-to-all-done.2.state, f32[8,8,256]{2,1,0:T(8,128)S(1)} %copy-done.2, f32[256,256]{1,0:T(8,128)S(1)} %select_maximum_fusion.operator, f32[8,256,256]{2,1,0:T(8,128)} %get-tuple-element.7.refs_0_), custom_call_target="tpu_custom_call", output_to_operand_aliasing={{0}: (3, {})} | custom-call | flops 13421772800 | bytes 3145728 | tf_op jit(solution)/shard_map/analyse/pallas_call | solution.py:189
  75.6 1.1 %all-to-all-done.1.refs_0_ = f32[32,4,8,256]{3,2,1,0:T(8,128)} async-done(((f32[32,4,8,256]{3,2,1,0:T(8,128)}), f32[32,4,8,256]{3,2,1,0:T(8,128)}, u32[]{:S(2)}, u32[]{:S(2)}) %all-to-all-start.1) | async-done | bytes 1048608 | tf_op jit(solution)/shard_map/all_to_all | solution.py:258
  76.6 23.4 %all_to_all.20.refs_1_ = f32[32,4,8,256]{3,2,1,0:T(8,128)} all-to-all(f32[32,4,8,256]{3,2,1,0:T(8,128)S(1)} %get-tuple-element.8), channel_id=1, replica_groups=mesh['mem'=32,'band'=4] {'mem'}, dimensions={0} | all-to-all | bytes 2097152 | tf_op jit(solution)/shard_map/all_to_all | solution.py:258
  100.0 3.5 %scatter.1 = f32[2048,256]{1,0:T(8,128)} custom-call(s32[256]{0:T(256)} %bitcast.15, f32[32,4,8,256]{3,2,1,0:T(8,128)} %all-to-all-done.1.refs_0_, f32[32,4,8,256]{3,2,1,0:T(8,128)} %all_to_all.20.refs_1_), custom_call_target="tpu_custom_call" | custom-call | tf_op jit(solution)/shard_map/scatter/pallas_call | solution.py:260
  (1 shorter events, 0.0 us)
Async XLA Ops:
  0.6 16.3 %copy-start = (s32[1,256,512]{2,1,0:T(8,128)S(1)}, s32[1,256,512]{2,1,0:T(8,128)}, u32[]{:S(2)}) copy-start(s32[1,256,512]{2,1,0:T(8,128)} %param.10) | copy-start | bytes 1572868
  4.0 26.8 %all-to-all-start = ((f32[32,4,8,256]{3,2,1,0:T(8,128)}), f32[32,4,8,256]{3,2,1,0:T(8,128)S(1)}, u32[]{:S(2)}, u32[]{:S(2)}) async-start(f32[32,4,8,256]{3,2,1,0:T(8,128)} %gather.2), calls=%async_computation | async-start | bytes 2097152 | tf_op jit(solution)/shard_map/all_to_all | solution.py:255
  13.6 6.1 %copy-start.3 = (f32[128,128]{1,0:T(8,128)S(1)}, f32[128,128]{1,0:T(8,128)}, u32[]{:S(2)}) copy-start(f32[128,128]{1,0:T(8,128)} %param.8) | copy-start | bytes 196612
  19.6 15.1 %copy-start.2 = (f32[8,8,256]{2,1,0:T(8,128)S(1)}, f32[8,8,256]{2,1,0:T(8,128)}, u32[]{:S(2)}) copy-start(f32[8,8,256]{2,1,0:T(8,128)} %slots.1.sums) | copy-start | bytes 196612
  30.7 21.3 %all-to-all-start.2 = ((f32[32,4,8,256]{3,2,1,0:T(8,128)}), f32[32,4,8,256]{3,2,1,0:T(8,128)S(1)}, u32[]{:S(2)}, u32[]{:S(2)}) async-start(f32[32,4,8,256]{3,2,1,0:T(8,128)} %gather.3), calls=%async_computation.2 | async-start | bytes 2097152 | tf_op jit(solution)/shard_map/all_to_all | solution.py:255
  50.9 1.0 copy-start.1
  52.0 24.6 %all-to-all-start.1 = ((f32[32,4,8,256]{3,2,1,0:T(8,128)}), f32[32,4,8,256]{3,2,1,0:T(8,128)}, u32[]{:S(2)}, u32[]{:S(2)}) async-start(f32[32,4,8,256]{3,2,1,0:T(8,128)} %copy-done.1), calls=%async_computation.1 | async-start | bytes 2097152 | tf_op jit(solution)/shard_map/all_to_all | solution.py:258

commit v4 on v3

--- a/solution.py
+++ b/solution.py
@@ -124,8 +124,8 @@
     return new_mats, new_roots
 
 
-def analyse_kernel(members, doubles, first, state, sums, operator, *refs):
-    transform_out, updated, transform, leave = refs[-4:]
+def analyse_kernel(members, doubles, first, last, state, sums, operator, *refs):
+    transform_out, updated_out, transform, leave, updated = (refs + (refs[-3],))[-5:] if last else refs[-5:]
     n = transform.shape[0]
     cells = state.shape[3]
     every = range(n)
@@ -168,9 +168,13 @@
         shift = mean + jnp.sum(pert * weight, axis=0, keepdims=True)
         result = shift + scale * product(split(root, 2), split(pert, 2))
         updated[:, i] = result.reshape(updated.shape[0], updated.shape[2], cells)
-    copy = pltpu.make_async_copy(transform, transform_out.at[pl.ds(first, n)], leave)
-    copy.start()
-    copy.wait()
+    copies = [pltpu.make_async_copy(transform, transform_out.at[pl.ds(first, n)], leave.at[0])]
+    if not last:
+        copies.append(pltpu.make_async_copy(updated, updated_out, leave.at[1]))
+    for copy in copies:
+        copy.start()
+    for copy in copies:
+        copy.wait()
 
 
 def analyse(chunk, chunks, state, sums, operator, transform):
@@ -179,6 +183,7 @@
     anywhere = pl.BlockSpec(memory_space=pl.ANY)
     vmem = pl.BlockSpec(memory_space=pltpu.VMEM)
     first = chunk * per_chunk
+    last = chunk == chunks - 1
     in_specs = [vmem, vmem, vmem]
     args = [pltpu.with_memory_space_constraint(state, pltpu.VMEM), sums, operator]
     aliases = {}
@@ -187,14 +192,15 @@
         args.append(transform)
         aliases = {3: 0}
     return pl.pallas_call(
-        functools.partial(analyse_kernel, members, 6, first),
+        functools.partial(analyse_kernel, members, 6, first, last),
         in_specs=in_specs,
-        out_specs=[anywhere, vmem],
+        out_specs=[anywhere, vmem if last else anywhere],
         out_shape=[
             jax.ShapeDtypeStruct((per_chunk * chunks, members, members), F),
-            pltpu.VMEM(state.shape, F),
+            pltpu.VMEM(state.shape, F) if last else pltpu.HBM(state.shape, F),
         ],
-        scratch_shapes=[pltpu.VMEM((per_chunk, members, members), F), pltpu.SemaphoreType.DMA],
+        scratch_shapes=[pltpu.VMEM((per_chunk, members, members), F), pltpu.SemaphoreType.DMA((2,))]
+        + ([] if last else [pltpu.VMEM(state.shape, F)]),
         input_output_aliases=aliases,
         compiler_params=pltpu.CompilerParams(vmem_limit_bytes=ANALYSE_VMEM),
         cost_estimate=pl.CostEstimate(

time: 104 us -> 104 us (level)
  transfers between devices with their start and end apart: 3 -> 3, of which waited for: 3 -> 3; matrix products, arithmetic and copies ran while one was open for 1% -> 1% of each run, Pallas kernels for 36% -> 37%
where the time goes in v4:
time: 104 us; the launch traced here: 103 us
  Pallas kernels  45.1 us (43%)
  blocking collectives  23.4 us (22%)
  starting transfers between devices  20.5 us (20%)
  waiting for transfers between devices  12.8 us (12%)
    pallas_call x2, Pallas kernels, analyse(): pl.pallas_call(functools.partial(analyse_kernel, members, 6, first, last)...  32.8 us
    all_to_all x1, blocking collectives, local(): returned.append(lax.all_to_all(updated, 'mem', 0, 0, tiled=True))  23.4 us
    all_to_all x2, starting transfers between devices, local(): states = [lax.all_to_all(x, 'mem', 0, 0, tiled=True) for x in listed]  13.6 us
    all_to_all x2, waiting for transfers between devices, local(): states = [lax.all_to_all(x, 'mem', 0, 0, tiled=True) for x in listed]  11.7 us
    all_to_all x1, starting transfers between devices, local(): returned.append(lax.all_to_all(updated, 'mem', 0, 0, tiled=True))  6.92 us
    pallas_call x2, Pallas kernels, local(): pl.pallas_call(functools.partial(gather_kernel, c, per_worker), grid=(lan...  6.64 us
    pallas_call x1, Pallas kernels, local(): pl.pallas_call(functools.partial(scatter_kernel, CHUNKS), grid=(lanes,),...  3.52 us
    pallas_call x1, Pallas kernels, local(): pl.pallas_call(slots_kernel, in_specs=[smem, vmem, vmem, vmem], out_specs...  2.12 us
  transfers between devices with their start and end apart: 3, of which 3 were waited for; matrix products, arithmetic and copies ran while one was open for 1% of the time, Pallas kernels for 37%

profile of v4, /device:TPU:1, one launch (start us, length us, event | category | flops | bytes accessed | tf_op | source)
XLA Modules:
  0.0 103.1 jit_solution(4595874461917829902)
XLA Ops:
  0.6 0.0 copy-start
  0.6 3.3 %gather.2 = f32[32,4,8,256]{3,2,1,0:T(8,128)} custom-call(s32[256]{0:T(256)} %bitcast.13, f32[2048,256]{1,0:T(8,128)} %bitcast.8), custom_call_target="tpu_custom_call" | custom-call | bytes 4194304 | tf_op jit(solution)/shard_map/gather/pallas_call | solution.py:232
  4.0 9.6 %all-to-all-start = ((f32[32,4,8,256]{3,2,1,0:T(8,128)}), f32[32,4,8,256]{3,2,1,0:T(8,128)S(1)}, u32[]{:S(2)}, u32[]{:S(2)}) async-start(f32[32,4,8,256]{3,2,1,0:T(8,128)} %gather.2), calls=%async_computation | async-start | bytes 2097152 | tf_op jit(solution)/shard_map/all_to_all | solution.py:261
  13.6 0.0 copy-start.2
  13.6 3.3 %gather.3 = f32[32,4,8,256]{3,2,1,0:T(8,128)} custom-call(s32[256]{0:T(256)} %bitcast.14, f32[2048,256]{1,0:T(8,128)} %bitcast.9), custom_call_target="tpu_custom_call" | custom-call | bytes 4194304 | tf_op jit(solution)/shard_map/gather/pallas_call | solution.py:232
  16.9 0.0 copy-done
  16.9 0.6 dynamic-slice_bitcast_fusion.index
  17.5 2.1 %slots.1.sums = f32[8,8,256]{2,1,0:T(8,128)} custom-call(s32[1,8]{1,0:T(1,128)} %count.1, s32[8,512]{1,0:T(8,128)} %dynamic-slice_bitcast_fusion.index, f32[8,512]{1,0:T(8,128)} %bitcast.11, f32[8,512]{1,0:T(8,128)} %bitcast.12), custom_call_target="tpu_custom_call" | custom-call | tf_op jit(solution)/shard_map/slots/pallas_call | solution.py:246
  19.6 0.0 copy-done.2
  19.7 0.0 copy-start.1
  19.7 11.1 %all-to-all-done.state = f32[32,4,8,256]{3,2,1,0:T(8,128)S(1)} async-done(((f32[32,4,8,256]{3,2,1,0:T(8,128)}), f32[32,4,8,256]{3,2,1,0:T(8,128)S(1)}, u32[]{:S(2)}, u32[]{:S(2)}) %all-to-all-start) | async-done | bytes 1048608 | tf_op jit(solution)/shard_map/all_to_all | solution.py:261
  30.7 4.0 %all-to-all-start.2 = ((f32[32,4,8,256]{3,2,1,0:T(8,128)}), f32[32,4,8,256]{3,2,1,0:T(8,128)S(1)}, u32[]{:S(2)}, u32[]{:S(2)}) async-start(f32[32,4,8,256]{3,2,1,0:T(8,128)} %gather.3), calls=%async_computation.2 | async-start | bytes 2097152 | tf_op jit(solution)/shard_map/all_to_all | solution.py:261
  34.7 0.0 copy-done.1
  34.7 16.6 %analyse.2 = (f32[8,256,256]{2,1,0:T(8,128)}, f32[32,4,8,256]{3,2,1,0:T(8,128)}) custom-call(f32[32,4,8,256]{3,2,1,0:T(8,128)S(1)} %all-to-all-done.state, f32[8,8,256]{2,1,0:T(8,128)S(1)} %copy-done.1, f32[256,256]{1,0:T(8,128)S(1)} %select_maximum_fusion.operator), custom_call_target="tpu_custom_call" | custom-call | flops 13421772800 | bytes 3145728 | tf_op jit(solution)/shard_map/analyse/pallas_call | solution.py:194
  51.4 0.7 all-to-all-done.2.state
  52.0 6.9 %all-to-all-start.1 = ((f32[32,4,8,256]{3,2,1,0:T(8,128)}), f32[32,4,8,256]{3,2,1,0:T(8,128)}, u32[]{:S(2)}, u32[]{:S(2)}) async-start(f32[32,4,8,256]{3,2,1,0:T(8,128)} %get-tuple-element.6), calls=%async_computation.1 | async-start | bytes 2097152 | tf_op jit(solution)/shard_map/all_to_all | solution.py:264
  58.9 16.2 %analyse.3 = (f32[8,256,256]{2,1,0:T(8,128)}, f32[32,4,8,256]{3,2,1,0:T(8,128)S(1)}) custom-call(f32[32,4,8,256]{3,2,1,0:T(8,128)S(1)} %all-to-all-done.2.state, f32[8,8,256]{2,1,0:T(8,128)S(1)} %copy-done.1, f32[256,256]{1,0:T(8,128)S(1)} %select_maximum_fusion.operator, f32[8,256,256]{2,1,0:T(8,128)} %get-tuple-element.7.refs_0_), custom_call_target="tpu_custom_call", output_to_operand_aliasing={{0}: (3, {})} | custom-call | flops 13421772800 | bytes 3145728 | tf_op jit(solution)/shard_map/analyse/pallas_call | solution.py:194
  75.1 1.1 %all-to-all-done.1.refs_0_ = f32[32,4,8,256]{3,2,1,0:T(8,128)} async-done(((f32[32,4,8,256]{3,2,1,0:T(8,128)}), f32[32,4,8,256]{3,2,1,0:T(8,128)}, u32[]{:S(2)}, u32[]{:S(2)}) %all-to-all-start.1) | async-done | bytes 1048608 | tf_op jit(solution)/shard_map/all_to_all | solution.py:264
  76.2 23.4 %all_to_all.20.refs_1_ = f32[32,4,8,256]{3,2,1,0:T(8,128)} all-to-all(f32[32,4,8,256]{3,2,1,0:T(8,128)S(1)} %get-tuple-element.8), channel_id=1, replica_groups=mesh['mem'=32,'band'=4] {'mem'}, dimensions={0} | all-to-all | bytes 2097152 | tf_op jit(solution)/shard_map/all_to_all | solution.py:264
  99.6 3.5 %scatter.1 = f32[2048,256]{1,0:T(8,128)} custom-call(s32[256]{0:T(256)} %bitcast.15, f32[32,4,8,256]{3,2,1,0:T(8,128)} %all-to-all-done.1.refs_0_, f32[32,4,8,256]{3,2,1,0:T(8,128)} %all_to_all.20.refs_1_), custom_call_target="tpu_custom_call" | custom-call | tf_op jit(solution)/shard_map/scatter/pallas_call | solution.py:266
  (1 shorter events, 0.0 us)
Async XLA Ops:
  0.6 16.3 %copy-start = (s32[1,256,512]{2,1,0:T(8,128)S(1)}, s32[1,256,512]{2,1,0:T(8,128)}, u32[]{:S(2)}) copy-start(s32[1,256,512]{2,1,0:T(8,128)} %param.10) | copy-start | bytes 1572868
  4.0 26.8 %all-to-all-start = ((f32[32,4,8,256]{3,2,1,0:T(8,128)}), f32[32,4,8,256]{3,2,1,0:T(8,128)S(1)}, u32[]{:S(2)}, u32[]{:S(2)}) async-start(f32[32,4,8,256]{3,2,1,0:T(8,128)} %gather.2), calls=%async_computation | async-start | bytes 2097152 | tf_op jit(solution)/shard_map/all_to_all | solution.py:261
  13.6 6.1 %copy-start.2 = (f32[128,128]{1,0:T(8,128)S(1)}, f32[128,128]{1,0:T(8,128)}, u32[]{:S(2)}) copy-start(f32[128,128]{1,0:T(8,128)} %param.8) | copy-start | bytes 196612
  19.7 15.1 %copy-start.1 = (f32[8,8,256]{2,1,0:T(8,128)S(1)}, f32[8,8,256]{2,1,0:T(8,128)}, u32[]{:S(2)}) copy-start(f32[8,8,256]{2,1,0:T(8,128)} %slots.1.sums) | copy-start | bytes 196612
  30.7 21.3 %all-to-all-start.2 = ((f32[32,4,8,256]{3,2,1,0:T(8,128)}), f32[32,4,8,256]{3,2,1,0:T(8,128)S(1)}, u32[]{:S(2)}, u32[]{:S(2)}) async-start(f32[32,4,8,256]{3,2,1,0:T(8,128)} %gather.3), calls=%async_computation.2 | async-start | bytes 2097152 | tf_op jit(solution)/shard_map/all_to_all | solution.py:261
  52.0 24.1 %all-to-all-start.1 = ((f32[32,4,8,256]{3,2,1,0:T(8,128)}), f32[32,4,8,256]{3,2,1,0:T(8,128)}, u32[]{:S(2)}, u32[]{:S(2)}) async-start(f32[32,4,8,256]{3,2,1,0:T(8,128)} %get-tuple-element.6), calls=%async_computation.1 | async-start | bytes 2097152 | tf_op jit(solution)/shard_map/all_to_all | solution.py:264
